TPU v7x, 32 devices: a whole 2x2x4 slice. The times are simulated.
32 devices in a mesh: section: 2 (over y), ctx: 4 (over z), dp: 4 (over x, core).
Axes of the slice: x: 2, y: 2, z: 4, core: 2. Of those that a mesh axis runs over, the one named last changes fastest.
Arguments:
- cotangent: bfloat16 [4, 512, 4096], P('dp', 'ctx'), may hold values from -6 to 6
- activations: bfloat16 [2, 4, 512, 4096], P('section', 'dp', 'ctx'), may hold values from -6 to 6
- gate_values: bfloat16 [2, 4, 512, 4096], P('section', 'dp', 'ctx'), may hold values from -6 to 6
- residue: float32 [2, 4096], P('section'), may hold values from -1 to 1
- skip_gain: float32 [2, 4096], P('section'), may hold values from -3 to 3
- decay_rate: float32 [2, 4096], P('section'), may hold values from 9.765625e-05 to 0.03
Outputs:
- input_grads: bfloat16 [2, 4, 512, 4096], P('section', 'dp', 'ctx')
- grad_residue: float32 [2, 4096], P('section')
- grad_skip: float32 [2, 4096], P('section')
All inputs are finite; a program needn't handle non-finite values.
Results may differ from a plain program's by a relative error of at most 0.0079.
Values may be sent and summed in bfloat16 or wider, within the bound.
A program may use at most 64 MiB of HBM per device.

v0:
```python
import functools
import math

import jax
import jax.numpy as jnp
from jax import lax
from jax.experimental import pallas as pl
from jax.experimental.pallas import tpu as pltpu
from jax.sharding import PartitionSpec as P

MESH = pl.DeviceIdType.MESH
F32 = jnp.float32
BF16 = jnp.bfloat16
WIDTH = 512


def kernel(sizes, cot, act, gate, residue, skip, rate, out, g_res, g_skip,
           cot_v, act_v, gate_v, inc_v, recv_v, out_v, y_v, pos_v, neg_v, pos_up, neg_up, tri,
           res_up, skip_up, rate_up, pre_out, pre_in, msg, tot,
           load_sem, store_sem, par_s, par_r, y_s, y_r, pre_s, pre_r, msg_s, msg_r, tot_s, tot_r):
    sections, n_ctx, n_dp, width, factor = sizes
    tokens, channels = cot.shape
    chunks = channels // width
    sec, ctx, dp = (lax.axis_index(a) for a in ("section", "ctx", "dp"))
    is_top = sec == sections - 1
    is_second = sec == sections - 2

    loads = [
        pltpu.make_async_copy(src, dst, load_sem.at[n])
        for n, (src, dst) in enumerate(((gate, gate_v), (cot, cot_v), (act, act_v)))
    ]
    for load in loads:
        load.start()

    barrier = pltpu.get_barrier_semaphore()
    for j in range(1, n_ctx):
        pl.semaphore_signal(barrier, inc=1, device_id={"ctx": lax.rem(ctx + j, n_ctx)}, device_id_type=MESH)
    for j in range(1, n_dp):
        pl.semaphore_signal(barrier, inc=1, device_id={"dp": lax.rem(dp + j, n_dp)}, device_id_type=MESH)

    @pl.when(sec > 0)
    def _():
        pl.semaphore_signal(barrier, inc=1, device_id={"section": sec - 1}, device_id_type=MESH)

    @pl.when(sec < sections - 1)
    def _():
        pl.semaphore_signal(barrier, inc=1, device_id={"section": sec + 1}, device_id_type=MESH)

    ends = jnp.where(sec > 0, 1, 0) + jnp.where(sec < sections - 1, 1, 0)
    pl.semaphore_wait(barrier, n_ctx - 1 + n_dp - 1 + ends)

    def cols(i):
        return pl.ds(pl.multiple_of(i * width, width), width)

    def below(src, dst, send, recv):
        return pltpu.make_async_remote_copy(
            src_ref=src, dst_ref=dst, send_sem=send, recv_sem=recv,
            device_id={"section": lax.rem(sec + sections - 1, sections)}, device_id_type=MESH)

    def params_down():
        return [
            below(src, dst, par_s.at[n], par_r.at[n])
            for n, (src, dst) in enumerate(((residue, res_up), (skip, skip_up), (rate, rate_up)))
        ]

    def gate_down(i):
        return below(gate.at[:, cols(i)], recv_v.at[:, cols(i)], y_s.at[i], y_r.at[i])

    def out_down(i):
        return below(out_v.at[:, cols(i)], recv_v.at[:, cols(i)], y_s.at[i], y_r.at[i])

    def prefix_down(i):
        return below(pre_out.at[:, cols(i)], pre_in.at[:, cols(i)], pre_s.at[i], pre_r.at[i])

    def message(j, i, slot):
        peer = lax.rem(ctx + j, n_ctx)
        return pltpu.make_async_remote_copy(
            src_ref=msg.at[slot, :, cols(i)], dst_ref=msg.at[slot, :, cols(i)],
            send_sem=msg_s.at[j, i], recv_sem=msg_r.at[slot, i],
            device_id={"ctx": peer}, device_id_type=MESH)

    def total(j, i, slot):
        peer = lax.rem(dp + j, n_dp)
        return pltpu.make_async_remote_copy(
            src_ref=tot.at[slot, :, cols(i)], dst_ref=tot.at[slot, :, cols(i)],
            send_sem=tot_s.at[j, i], recv_sem=tot_r.at[slot, i],
            device_id={"dp": peer}, device_id_type=MESH)

    def stored(i):
        return pltpu.make_async_copy(out_v.at[:, cols(i)], out.at[:, cols(i)], store_sem.at[i])

    half = (chunks + 1) // 2

    @pl.when(is_top)
    def _():
        for copy in params_down():
            copy.start()
        pl.loop(0, half)(lambda i: gate_down(i).start())

    at = lax.broadcasted_iota(jnp.int32, (tokens, tokens), 0)
    of = lax.broadcasted_iota(jnp.int32, (tokens, tokens), 1)
    upper = jnp.where(of >= at, 1.0, 0.0).astype(BF16)
    tri[:, :tokens] = upper
    tri[:, tokens:] = upper

    def tables(rate_ref, pos_ref, neg_ref):
        @pl.loop(0, chunks)
        def _(i):
            steps = lax.broadcasted_iota(jnp.int32, (tokens, width), 0).astype(F32)
            powers = steps * rate_ref[:, cols(i)]
            pos_ref[:, cols(i)] = jnp.exp(powers)
            neg_ref[:, cols(i)] = jnp.exp(-powers)

    def suffix_sums(scaled):
        high = scaled.astype(BF16)
        low = (scaled - high.astype(F32)).astype(BF16)
        both = jnp.concatenate([high, low], axis=0)
        return jnp.dot(tri[...], both, preferred_element_type=F32)

    def weigh(incoming, gates):
        return (incoming * gates).astype(BF16).astype(F32)

    def result(incoming, weighted, sums, row, pos, res, gain):
        carried = (pos * (sums + row)).astype(BF16).astype(F32)
        return (incoming + (res * carried + gain * weighted)).astype(BF16)

    def arrive(i):
        gate_down(i).wait_recv()
        c = cols(i)

        @pl.when(is_second)
        def _():
            prefix_down(i).wait_recv()
            incoming = cot_v[:, c].astype(F32)
            weighted = weigh(incoming, recv_v[:, c].astype(F32))
            sums = suffix_sums(neg_up[:, c] * weighted)
            inc_v[:, c] = result(incoming, weighted, sums, pre_in[:, c], pos_up[:, c], res_up[:, c], skip_up[:, c])

        if sections > 2:
            @pl.when(jnp.logical_not(is_second))
            def _():
                inc_v[:, c] = recv_v[:, c]

    def front(i, inc_ref):
        c = cols(i)
        weighted = weigh(inc_ref[:, c].astype(F32), gate_v[:, c].astype(F32))
        sums = suffix_sums(neg_v[:, c] * weighted)
        y_v[:, c] = sums
        saved = act_v[:, c].astype(F32)
        lifted = saved * pos_v[:, c]
        fade = jnp.exp(rate[:, c] * -float(tokens))
        msg[ctx, 0:1, c] = sums[0:1]
        msg[ctx, 1:2, c] = jnp.sum(lifted * sums, axis=0, keepdims=True)
        msg[ctx, 2:3, c] = jnp.sum(lifted, axis=0, keepdims=True) * fade
        msg[ctx, 3:4, c] = jnp.sum(saved * weighted, axis=0, keepdims=True)
        for j in range(1, n_ctx):
            message(j, i, ctx).start()

    def back(i, inc_ref, top):
        c = cols(i)
        for j in range(1, n_ctx):
            message(j, i, lax.rem(ctx + j, n_ctx)).wait_recv()
        fade = jnp.exp(rate[:, c] * -float(tokens))
        after = jnp.zeros((1, width), F32)
        entering, total_res, total_skip = after, after, after
        for k in reversed(range(n_ctx)):
            total_res += msg[k, 1:2, c] + msg[k, 2:3, c] * after
            total_skip += msg[k, 3:4, c]
            entering = jnp.where(ctx == k, after, entering)
            after = msg[k, 0:1, c] + fade * after
        tot[dp, 0:1, c] = total_res
        tot[dp, 1:2, c] = total_skip
        for j in range(1, n_dp):
            total(j, i, dp).start()
        row = fade * entering
        if top:
            pre_out[:, c] = row
            prefix_down(i).start()
        incoming = inc_ref[:, c].astype(F32)
        weighted = weigh(incoming, gate_v[:, c].astype(F32))
        out_v[:, c] = result(incoming, weighted, y_v[:, c], row, pos_v[:, c], residue[:, c], skip[:, c])
        stored(i).start()
        if sections > 2 and not top:
            @pl.when(sec > 0)
            def _():
                out_down(i).start()

    tables(rate, pos_v, neg_v)
    for load in loads:
        load.wait()

    @pl.when(is_top)
    def _():
        pl.loop(0, chunks)(lambda i: front(i, cot_v))
        pl.loop(0, chunks)(lambda i: back(i, cot_v, True))
        pl.loop(half, chunks)(lambda i: gate_down(i).start())

    @pl.when(jnp.logical_not(is_top))
    def _():
        @pl.when(is_second)
        def _():
            for copy in params_down():
                copy.wait_recv()
            tables(rate_up, pos_up, neg_up)

        arrive(0)
        front(0, inc_v)

        @pl.loop(1, chunks)
        def _(i):
            arrive(i)
            front(i, inc_v)
            back(i - 1, inc_v, False)

        back(chunks - 1, inc_v, False)

    @pl.loop(0, chunks)
    def _(i):
        for j in range(1, n_dp):
            total(j, i, lax.rem(dp + j, n_dp)).wait_recv()
        c = cols(i)
        sums = tot[0, :, c]
        for k in range(1, n_dp):
            sums += tot[k, :, c]
        sums *= factor
        g_res[:, c] = sums[0:1]
        g_skip[:, c] = sums[1:2]

    @pl.loop(0, chunks)
    def _(i):
        for j in range(1, n_ctx):
            message(j, i, ctx).wait_send()
        for j in range(1, n_dp):
            total(j, i, dp).wait_send()
        stored(i).wait()

    @pl.when(is_top)
    def _():
        for copy in params_down():
            copy.wait_send()

        @pl.loop(0, chunks)
        def _(i):
            prefix_down(i).wait_send()
            gate_down(i).wait_send()

    if sections > 2:
        @pl.when(jnp.logical_and(sec > 0, jnp.logical_not(is_top)))
        def _():
            pl.loop(0, chunks)(lambda i: out_down(i).wait_send())


def on_device(cotangent, activations, gate_values, residue, skip_gain, decay_rate):
    sections, n_ctx, n_dp = (lax.axis_size(a) for a in ("section", "ctx", "dp"))
    tokens, channels = cotangent.shape[-2:]
    factor = 1.0 / math.sqrt(n_dp * n_ctx * tokens)
    width = math.gcd(WIDTH, channels)
    chunks = channels // width
    sizes = (sections, n_ctx, n_dp, width, factor)
    block = (tokens, channels)
    anywhere = pl.BlockSpec(memory_space=pl.ANY)
    inside = pl.BlockSpec(memory_space=pltpu.VMEM)
    row = jax.ShapeDtypeStruct((1, channels), F32)
    dma = pltpu.SemaphoreType.DMA
    result, g_res, g_skip = pl.pallas_call(
        functools.partial(kernel, sizes),
        out_shape=(jax.ShapeDtypeStruct(block, BF16), row, row),
        in_specs=[anywhere] * 3 + [inside] * 3,
        out_specs=(anywhere, inside, inside),
        scratch_shapes=[pltpu.VMEM(block, BF16)] * 6
        + [pltpu.VMEM(block, F32)] * 5
        + [pltpu.VMEM((tokens, 2 * tokens), BF16)]
        + [pltpu.VMEM((1, channels), F32)] * 5
        + [pltpu.VMEM((n_ctx, 4, channels), F32), pltpu.VMEM((n_dp, 2, channels), F32)]
        + [dma((3,)), dma((chunks,)), dma((3,)), dma((3,))]
        + [dma((chunks,))] * 4
        + [dma((n_ctx, chunks))] * 2
        + [dma((n_dp, chunks))] * 2,
        compiler_params=pltpu.CompilerParams(
            collective_id=0, has_side_effects=True, vmem_limit_bytes=40 * 1024 * 1024),
    )(cotangent.reshape(block), activations.reshape(block), gate_values.reshape(block),
      residue, skip_gain, decay_rate)
    return result.reshape(activations.shape), g_res, g_skip


def solution(mesh):
    return jax.shard_map(
        on_device,
        mesh=mesh,
        in_specs=(
            P("dp", "ctx", None),
            P("section", "dp", "ctx", None),
            P("section", "dp", "ctx", None),
            P("section", None),
            P("section", None),
            P("section", None),
        ),
        out_specs=(P("section", "dp", "ctx", None), P("section", None), P("section", None)),
        check_vma=False,
    )
```

profile of v0, /device:TPU:0, one launch (start us, length us, event | category | flops | bytes accessed | tf_op | source)
XLA Modules:
  0.0 52.1 jit_solution(8462576603439474808)
XLA Ops:
  0.6 0.0 copy-start
  0.6 1.2 %copy-done = bf16[1,128,4096]{2,1,0:T(8,128)(2,1)S(1)} copy-done((bf16[1,128,4096]{2,1,0:T(8,128)(2,1)S(1)}, bf16[1,128,4096]{2,1,0:T(8,128)(2,1)}, u32[]{:S(2)}) %copy-start) | copy-done | bytes 1048600
  1.9 0.0 copy-start.1
  1.9 1.2 %copy-done.1 = bf16[1,1,128,4096]{3,2,1,0:T(8,128)(2,1)S(1)} copy-done((bf16[1,1,128,4096]{3,2,1,0:T(8,128)(2,1)S(1)}, bf16[1,1,128,4096]{3,2,1,0:T(8,128)(2,1)}, u32[]{:S(2)}) %copy-start.1) | copy-done | bytes 1048600
  3.1 0.0 copy-start.2
  3.1 1.2 %copy-done.2 = bf16[1,1,128,4096]{3,2,1,0:T(8,128)(2,1)S(1)} copy-done((bf16[1,1,128,4096]{3,2,1,0:T(8,128)(2,1)S(1)}, bf16[1,1,128,4096]{3,2,1,0:T(8,128)(2,1)}, u32[]{:S(2)}) %copy-start.2) | copy-done | bytes 1048600
  4.3 0.0 copy-start.3
  4.3 0.7 %copy-done.3 = f32[1,4096]{1,0:T(1,128)S(1)} copy-done((f32[1,4096]{1,0:T(1,128)S(1)}, f32[1,4096]{1,0:T(1,128)}, u32[]{:S(2)}) %copy-start.3) | copy-done | bytes 16408
  5.0 0.0 copy-start.4
  5.0 0.7 %copy-done.4 = f32[1,4096]{1,0:T(1,128)S(1)} copy-done((f32[1,4096]{1,0:T(1,128)S(1)}, f32[1,4096]{1,0:T(1,128)}, u32[]{:S(2)}) %copy-start.4) | copy-done | bytes 16408
  5.7 0.0 copy-start.5
  5.7 0.7 %copy-done.5 = f32[1,4096]{1,0:T(1,128)S(1)} copy-done((f32[1,4096]{1,0:T(1,128)S(1)}, f32[1,4096]{1,0:T(1,128)}, u32[]{:S(2)}) %copy-start.5) | copy-done | bytes 16408
  6.5 43.4 %shard_map.85 = (bf16[128,4096]{1,0:T(8,128)(2,1)S(1)}, f32[1,4096]{1,0:T(1,128)S(1)}, f32[1,4096]{1,0:T(1,128)S(1)}) custom-call(bf16[128,4096]{1,0:T(8,128)(2,1)S(1)} %bitcast.4, bf16[128,4096]{1,0:T(8,128)(2,1)S(1)} %bitcast.5, bf16[128,4096]{1,0:T(8,128)(2,1)S(1)} %bitcast.6, f32[1,4096]{1,0:T(1,128)S(1)} %copy-done.3, f32[1,4096]{1,0:T(1,128)S(1)} %copy-done.4, ...), custom_call_target="tpu_custom_call" | custom-call | tf_op jit(solution)/shard_map/pallas_call | solution.py:265
  49.9 1.0 %copy.12 = bf16[1,1,128,4096]{3,2,1,0:T(8,128)(2,1)} copy(bf16[1,1,128,4096]{3,2,1,0:T(8,128)(2,1)S(1)} %bitcast.7) | data formatting | bytes 2097152
  50.9 0.6 %copy.13 = f32[1,4096]{1,0:T(1,128)} copy(f32[1,4096]{1,0:T(1,128)S(1)} %get-tuple-element.13) | data formatting | bytes 32768
  51.5 0.6 %copy.14 = f32[1,4096]{1,0:T(1,128)} copy(f32[1,4096]{1,0:T(1,128)S(1)} %get-tuple-element.14) | data formatting | bytes 32768
Async XLA Ops:
  0.6 1.2 %copy-start = (bf16[1,128,4096]{2,1,0:T(8,128)(2,1)S(1)}, bf16[1,128,4096]{2,1,0:T(8,128)(2,1)}, u32[]{:S(2)}) copy-start(bf16[1,128,4096]{2,1,0:T(8,128)(2,1)} %param.6) | copy-start | bytes 3145732
  1.9 1.2 %copy-start.1 = (bf16[1,1,128,4096]{3,2,1,0:T(8,128)(2,1)S(1)}, bf16[1,1,128,4096]{3,2,1,0:T(8,128)(2,1)}, u32[]{:S(2)}) copy-start(bf16[1,1,128,4096]{3,2,1,0:T(8,128)(2,1)} %param.7) | copy-start | bytes 3145732
  3.1 1.2 %copy-start.2 = (bf16[1,1,128,4096]{3,2,1,0:T(8,128)(2,1)S(1)}, bf16[1,1,128,4096]{3,2,1,0:T(8,128)(2,1)}, u32[]{:S(2)}) copy-start(bf16[1,1,128,4096]{3,2,1,0:T(8,128)(2,1)} %param.8) | copy-start | bytes 3145732
  4.3 0.7 %copy-start.3 = (f32[1,4096]{1,0:T(1,128)S(1)}, f32[1,4096]{1,0:T(1,128)}, u32[]{:S(2)}) copy-start(f32[1,4096]{1,0:T(1,128)} %residue.1) | copy-start | bytes 49156
  5.0 0.7 %copy-start.4 = (f32[1,4096]{1,0:T(1,128)S(1)}, f32[1,4096]{1,0:T(1,128)}, u32[]{:S(2)}) copy-start(f32[1,4096]{1,0:T(1,128)} %skip.1) | copy-start | bytes 49156
  5.7 0.7 %copy-start.5 = (f32[1,4096]{1,0:T(1,128)S(1)}, f32[1,4096]{1,0:T(1,128)}, u32[]{:S(2)}) copy-start(f32[1,4096]{1,0:T(1,128)} %rate.1) | copy-start | bytes 49156
where the time goes:
time: 52.5 us; the launch traced here: 52.1 us
  Pallas kernels  43.4 us (83%)
  local copies, waits for them, and re-layouts  8 us (15%)
  between operations  0.65 us (1%)
    pallas_call x1, Pallas kernels, on_device(): pl.pallas_call(functools.partial(kernel, sizes), out_shape=(jax.ShapeDtyp...  43.4 us
    unnamed x15, local copies, waits for them, and re-layouts  8 us

commit v1 on v0

--- a/solution.py
+++ b/solution.py
@@ -12,12 +12,14 @@
 F32 = jnp.float32
 BF16 = jnp.bfloat16
 WIDTH = 512
-
-
-def kernel(sizes, cot, act, gate, residue, skip, rate, out, g_res, g_skip,
+LEAD = 3
+LAG = 1
+
+
+def kernel(sizes, cot, act, gate, residue_h, skip_h, rate_h, out, g_res, g_skip,
            cot_v, act_v, gate_v, inc_v, recv_v, out_v, y_v, pos_v, neg_v, pos_up, neg_up, tri,
-           res_up, skip_up, rate_up, pre_out, pre_in, msg, tot,
-           load_sem, store_sem, par_s, par_r, y_s, y_r, pre_s, pre_r, msg_s, msg_r, tot_s, tot_r):
+           residue, skip, rate, res_up, skip_up, rate_up, pre_out, pre_in, heads, msg, tot,
+           load_sem, store_sem, par_s, par_r, y_s, y_r, pre_s, pre_r, head_s, head_r, msg_s, msg_r, tot_s, tot_r):
     sections, n_ctx, n_dp, width, factor = sizes
     tokens, channels = cot.shape
     chunks = channels // width
@@ -27,7 +29,8 @@
 
     loads = [
         pltpu.make_async_copy(src, dst, load_sem.at[n])
-        for n, (src, dst) in enumerate(((gate, gate_v), (cot, cot_v), (act, act_v)))
+        for n, (src, dst) in enumerate((
+            (gate, gate_v), (cot, cot_v), (rate_h, rate), (residue_h, residue), (skip_h, skip), (act, act_v)))
     ]
     for load in loads:
         load.start()
@@ -60,7 +63,7 @@
     def params_down():
         return [
             below(src, dst, par_s.at[n], par_r.at[n])
-            for n, (src, dst) in enumerate(((residue, res_up), (skip, skip_up), (rate, rate_up)))
+            for n, (src, dst) in enumerate(((residue_h, res_up), (skip_h, skip_up), (rate_h, rate_up)))
         ]
 
     def gate_down(i):
@@ -69,8 +72,14 @@
     def out_down(i):
         return below(out_v.at[:, cols(i)], recv_v.at[:, cols(i)], y_s.at[i], y_r.at[i])
 
-    def prefix_down(i):
-        return below(pre_out.at[:, cols(i)], pre_in.at[:, cols(i)], pre_s.at[i], pre_r.at[i])
+    def prefix_down():
+        return below(pre_out, pre_in, pre_s, pre_r)
+
+    def head(j, slot):
+        return pltpu.make_async_remote_copy(
+            src_ref=heads.at[slot], dst_ref=heads.at[slot],
+            send_sem=head_s.at[j], recv_sem=head_r.at[slot],
+            device_id={"ctx": lax.rem(ctx + j, n_ctx)}, device_id_type=MESH)
 
     def message(j, i, slot):
         peer = lax.rem(ctx + j, n_ctx)
@@ -89,13 +98,14 @@
     def stored(i):
         return pltpu.make_async_copy(out_v.at[:, cols(i)], out.at[:, cols(i)], store_sem.at[i])
 
-    half = (chunks + 1) // 2
+    lead = min(LEAD, chunks)
+    lag = min(LAG, chunks)
 
     @pl.when(is_top)
     def _():
         for copy in params_down():
             copy.start()
-        pl.loop(0, half)(lambda i: gate_down(i).start())
+        pl.loop(0, lead)(lambda i: gate_down(i).start())
 
     at = lax.broadcasted_iota(jnp.int32, (tokens, tokens), 0)
     of = lax.broadcasted_iota(jnp.int32, (tokens, tokens), 1)
@@ -130,7 +140,6 @@
 
         @pl.when(is_second)
         def _():
-            prefix_down(i).wait_recv()
             incoming = cot_v[:, c].astype(F32)
             weighted = weigh(incoming, recv_v[:, c].astype(F32))
             sums = suffix_sums(neg_up[:, c] * weighted)
@@ -141,26 +150,44 @@
             def _():
                 inc_v[:, c] = recv_v[:, c]
 
-    def front(i, inc_ref):
-        c = cols(i)
-        weighted = weigh(inc_ref[:, c].astype(F32), gate_v[:, c].astype(F32))
+    def fade_of(c):
+        return jnp.exp(rate[:, c] * -float(tokens))
+
+    def column_sum(values):
+        return jnp.sum(values, axis=0, keepdims=True)
+
+    def announce(i, *rows):
+        for n, row in enumerate(rows):
+            msg[ctx, n:n + 1, cols(i)] = row
+        for j in range(1, n_ctx):
+            message(j, i, ctx).start()
+
+    def whole_block(i):
+        c = cols(i)
+        incoming = cot_v[:, c].astype(F32)
+        weighted = weigh(incoming, gate_v[:, c].astype(F32))
+        sums = suffix_sums(neg_v[:, c] * weighted)
+        carried = (pos_v[:, c] * (sums + pre_out[:, c])).astype(BF16).astype(F32)
+        out_v[:, c] = (incoming + (residue[:, c] * carried + skip[:, c] * weighted)).astype(BF16)
+        stored(i).start()
+        saved = act_v[:, c].astype(F32)
+        none = jnp.zeros((1, width), F32)
+        announce(i, none, column_sum(saved * carried), none, column_sum(saved * weighted))
+
+    def front(i):
+        c = cols(i)
+        weighted = weigh(inc_v[:, c].astype(F32), gate_v[:, c].astype(F32))
         sums = suffix_sums(neg_v[:, c] * weighted)
         y_v[:, c] = sums
         saved = act_v[:, c].astype(F32)
         lifted = saved * pos_v[:, c]
-        fade = jnp.exp(rate[:, c] * -float(tokens))
-        msg[ctx, 0:1, c] = sums[0:1]
-        msg[ctx, 1:2, c] = jnp.sum(lifted * sums, axis=0, keepdims=True)
-        msg[ctx, 2:3, c] = jnp.sum(lifted, axis=0, keepdims=True) * fade
-        msg[ctx, 3:4, c] = jnp.sum(saved * weighted, axis=0, keepdims=True)
-        for j in range(1, n_ctx):
-            message(j, i, ctx).start()
-
-    def back(i, inc_ref, top):
+        announce(i, sums[0:1], column_sum(lifted * sums), column_sum(lifted) * fade_of(c), column_sum(saved * weighted))
+
+    def combine(i):
         c = cols(i)
         for j in range(1, n_ctx):
             message(j, i, lax.rem(ctx + j, n_ctx)).wait_recv()
-        fade = jnp.exp(rate[:, c] * -float(tokens))
+        fade = fade_of(c)
         after = jnp.zeros((1, width), F32)
         entering, total_res, total_skip = after, after, after
         for k in reversed(range(n_ctx)):
@@ -172,47 +199,88 @@
         tot[dp, 1:2, c] = total_skip
         for j in range(1, n_dp):
             total(j, i, dp).start()
-        row = fade * entering
-        if top:
-            pre_out[:, c] = row
-            prefix_down(i).start()
-        incoming = inc_ref[:, c].astype(F32)
+        return fade * entering
+
+    def back(i):
+        c = cols(i)
+        row = combine(i)
+        incoming = inc_v[:, c].astype(F32)
         weighted = weigh(incoming, gate_v[:, c].astype(F32))
         out_v[:, c] = result(incoming, weighted, y_v[:, c], row, pos_v[:, c], residue[:, c], skip[:, c])
         stored(i).start()
-        if sections > 2 and not top:
+        if sections > 2:
             @pl.when(sec > 0)
             def _():
                 out_down(i).start()
 
-    tables(rate, pos_v, neg_v)
-    for load in loads:
+    for load in loads[:-1]:
         load.wait()
 
     @pl.when(is_top)
     def _():
-        pl.loop(0, chunks)(lambda i: front(i, cot_v))
-        pl.loop(0, chunks)(lambda i: back(i, cot_v, True))
-        pl.loop(half, chunks)(lambda i: gate_down(i).start())
+        steps = lax.broadcasted_iota(jnp.int32, (tokens, width), 0).astype(F32)
+
+        @pl.loop(0, chunks)
+        def _(i):
+            c = cols(i)
+            factors = jnp.exp(-(steps * rate[:, c]))
+            neg_v[:, c] = factors
+            heads[ctx, 0:1, c] = column_sum(factors * weigh(cot_v[:, c].astype(F32), gate_v[:, c].astype(F32)))
+
+        for j in range(1, n_ctx):
+            head(j, ctx).start()
+
+        @pl.loop(0, chunks)
+        def _(i):
+            pos_v[:, cols(i)] = jnp.exp(steps * rate[:, cols(i)])
+
+        for j in range(1, n_ctx):
+            head(j, lax.rem(ctx + j, n_ctx)).wait_recv()
+
+        @pl.loop(0, chunks)
+        def _(i):
+            c = cols(i)
+            fade = fade_of(c)
+            after = jnp.zeros((1, width), F32)
+            entering = after
+            for k in reversed(range(n_ctx)):
+                entering = jnp.where(ctx == k, after, entering)
+                after = heads[k, :, c] + fade * after
+            pre_out[:, c] = fade * entering
+
+        prefix_down().start()
+        pl.loop(lead, chunks)(lambda i: gate_down(i).start())
+        loads[-1].wait()
+        pl.loop(0, chunks)(whole_block)
+
+        @pl.loop(0, chunks)
+        def _(i):
+            combine(i)
 
     @pl.when(jnp.logical_not(is_top))
     def _():
+        tables(rate, pos_v, neg_v)
+        loads[-1].wait()
+
         @pl.when(is_second)
         def _():
             for copy in params_down():
                 copy.wait_recv()
             tables(rate_up, pos_up, neg_up)
-
-        arrive(0)
-        front(0, inc_v)
-
-        @pl.loop(1, chunks)
+            prefix_down().wait_recv()
+
+        @pl.loop(0, lag)
         def _(i):
             arrive(i)
-            front(i, inc_v)
-            back(i - 1, inc_v, False)
-
-        back(chunks - 1, inc_v, False)
+            front(i)
+
+        @pl.loop(lag, chunks)
+        def _(i):
+            arrive(i)
+            front(i)
+            back(i - lag)
+
+        pl.loop(chunks - lag, chunks)(back)
 
     @pl.loop(0, chunks)
     def _(i):
@@ -238,10 +306,12 @@
     def _():
         for copy in params_down():
             copy.wait_send()
-
-        @pl.loop(0, chunks)
-        def _(i):
-            prefix_down(i).wait_send()
+        prefix_down().wait_send()
+        for j in range(1, n_ctx):
+            head(j, ctx).wait_send()
+
+        @pl.loop(0, chunks)
+        def _(i):
             gate_down(i).wait_send()
 
     if sections > 2:
@@ -259,25 +329,27 @@
     sizes = (sections, n_ctx, n_dp, width, factor)
     block = (tokens, channels)
     anywhere = pl.BlockSpec(memory_space=pl.ANY)
+    outside = pl.BlockSpec(memory_space=pltpu.HBM)
     inside = pl.BlockSpec(memory_space=pltpu.VMEM)
     row = jax.ShapeDtypeStruct((1, channels), F32)
     dma = pltpu.SemaphoreType.DMA
     result, g_res, g_skip = pl.pallas_call(
         functools.partial(kernel, sizes),
         out_shape=(jax.ShapeDtypeStruct(block, BF16), row, row),
-        in_specs=[anywhere] * 3 + [inside] * 3,
+        in_specs=[outside] * 6,
         out_specs=(anywhere, inside, inside),
         scratch_shapes=[pltpu.VMEM(block, BF16)] * 6
         + [pltpu.VMEM(block, F32)] * 5
         + [pltpu.VMEM((tokens, 2 * tokens), BF16)]
-        + [pltpu.VMEM((1, channels), F32)] * 5
+        + [pltpu.VMEM((1, channels), F32)] * 8
+        + [pltpu.VMEM((n_ctx, 1, channels), F32)]
         + [pltpu.VMEM((n_ctx, 4, channels), F32), pltpu.VMEM((n_dp, 2, channels), F32)]
-        + [dma((3,)), dma((chunks,)), dma((3,)), dma((3,))]
-        + [dma((chunks,))] * 4
+        + [dma((6,)), dma((chunks,)), dma((3,)), dma((3,)), dma((chunks,)), dma((chunks,)), dma, dma]
+        + [dma((n_ctx,))] * 2
         + [dma((n_ctx, chunks))] * 2
         + [dma((n_dp, chunks))] * 2,
         compiler_params=pltpu.CompilerParams(
-            collective_id=0, has_side_effects=True, vmem_limit_bytes=40 * 1024 * 1024),
+            collective_id=0, has_side_effects=True, vmem_limit_bytes=60 * 1024 * 1024),
     )(cotangent.reshape(block), activations.reshape(block), gate_values.reshape(block),
       residue, skip_gain, decay_rate)
     return result.reshape(activations.shape), g_res, g_skip

time: 52.5 us -> 45.8 us (0.87)
  local copies, waits for them, and re-layouts: 8 us -> 3.63 us
  Pallas kernels: 43.4 us -> 41.3 us
    unnamed x15 -> x7, local copies, waits for them, and re-layouts: 8 us -> 3.63 us
    pallas_call x1, Pallas kernels: 43.4 us -> 41.3 us  [on_device(): pl.pallas_call(functools.partial(kernel, sizes), out_shape=(jax.ShapeDtyp...]
where the time goes in v1:
time: 45.8 us; the launch traced here: 45.6 us
  Pallas kernels  41.3 us (90%)
  local copies, waits for them, and re-layouts  3.63 us (8%)
  between operations  0.65 us (1%)
    pallas_call x1, Pallas kernels, on_device(): pl.pallas_call(functools.partial(kernel, sizes), out_shape=(jax.ShapeDtyp...  41.3 us
    unnamed x7, local copies, waits for them, and re-layouts  3.63 us

profile of v1, /device:TPU:0, one launch (start us, length us, event | category | flops | bytes accessed | tf_op | source)
XLA Modules:
  0.0 45.6 jit_solution(6309176253262090159)
XLA Ops:
  0.6 41.3 %shard_map.85 = (bf16[128,4096]{1,0:T(8,128)(2,1)}, f32[1,4096]{1,0:T(1,128)}, f32[1,4096]{1,0:T(1,128)}) custom-call(bf16[128,4096]{1,0:T(8,128)(2,1)} %bitcast.4, bf16[128,4096]{1,0:T(8,128)(2,1)} %bitcast.5, bf16[128,4096]{1,0:T(8,128)(2,1)} %bitcast.6, f32[1,4096]{1,0:T(1,128)} %residue_h.1, f32[1,4096]{1,0:T(1,128)} %skip_h.1, f32[1,4096]{1,0:T(1,128)} %rate_h.1), custom_call_target="tpu_custom_call" | custom-call | tf_op jit(solution)/shard_map/pallas_call | solution.py:336
  42.0 0.0 copy-start.1
  42.0 2.3 %copy.12 = bf16[1,1,128,4096]{3,2,1,0:T(8,128)(2,1)} copy(bf16[1,1,128,4096]{3,2,1,0:T(8,128)(2,1)} %bitcast.7) | data formatting | bytes 2097152
  44.3 0.0 copy-done.1
  44.3 0.0 copy-start
  44.3 0.6 %copy.13 = f32[1,4096]{1,0:T(1,128)} copy(f32[1,4096]{1,0:T(1,128)S(1)} %copy-done.1) | data formatting | bytes 32768
  44.9 0.1 copy-done
  45.0 0.6 %copy.14 = f32[1,4096]{1,0:T(1,128)} copy(f32[1,4096]{1,0:T(1,128)S(1)} %copy-done) | data formatting | bytes 32768
Async XLA Ops:
  42.0 2.3 %copy-start.1 = (f32[1,4096]{1,0:T(1,128)S(1)}, f32[1,4096]{1,0:T(1,128)}, u32[]{:S(2)}) copy-start(f32[1,4096]{1,0:T(1,128)} %get-tuple-element.13) | copy-start | bytes 49156
  44.3 0.7 %copy-start = (f32[1,4096]{1,0:T(1,128)S(1)}, f32[1,4096]{1,0:T(1,128)}, u32[]{:S(2)}) copy-start(f32[1,4096]{1,0:T(1,128)} %get-tuple-element.14) | copy-start | bytes 49156

commit v2 on v1

--- a/solution.py
+++ b/solution.py
@@ -12,8 +12,8 @@
 F32 = jnp.float32
 BF16 = jnp.bfloat16
 WIDTH = 512
-LEAD = 3
-LAG = 1
+LEAD = 2
+LAG = 2
 
 
 def kernel(sizes, cot, act, gate, residue_h, skip_h, rate_h, out, g_res, g_skip,
@@ -88,11 +88,11 @@
             send_sem=msg_s.at[j, i], recv_sem=msg_r.at[slot, i],
             device_id={"ctx": peer}, device_id_type=MESH)
 
-    def total(j, i, slot):
+    def total(j, slot):
         peer = lax.rem(dp + j, n_dp)
         return pltpu.make_async_remote_copy(
-            src_ref=tot.at[slot, :, cols(i)], dst_ref=tot.at[slot, :, cols(i)],
-            send_sem=tot_s.at[j, i], recv_sem=tot_r.at[slot, i],
+            src_ref=tot.at[slot], dst_ref=tot.at[slot],
+            send_sem=tot_s.at[j], recv_sem=tot_r.at[slot],
             device_id={"dp": peer}, device_id_type=MESH)
 
     def stored(i):
@@ -197,8 +197,6 @@
             after = msg[k, 0:1, c] + fade * after
         tot[dp, 0:1, c] = total_res
         tot[dp, 1:2, c] = total_skip
-        for j in range(1, n_dp):
-            total(j, i, dp).start()
         return fade * entering
 
     def back(i):
@@ -282,10 +280,13 @@
 
         pl.loop(chunks - lag, chunks)(back)
 
+    for j in range(1, n_dp):
+        total(j, dp).start()
+    for j in range(1, n_dp):
+        total(j, lax.rem(dp + j, n_dp)).wait_recv()
+
     @pl.loop(0, chunks)
     def _(i):
-        for j in range(1, n_dp):
-            total(j, i, lax.rem(dp + j, n_dp)).wait_recv()
         c = cols(i)
         sums = tot[0, :, c]
         for k in range(1, n_dp):
@@ -298,9 +299,10 @@
     def _(i):
         for j in range(1, n_ctx):
             message(j, i, ctx).wait_send()
-        for j in range(1, n_dp):
-            total(j, i, dp).wait_send()
         stored(i).wait()
+
+    for j in range(1, n_dp):
+        total(j, dp).wait_send()
 
     @pl.when(is_top)
     def _():
@@ -347,7 +349,7 @@
         + [dma((6,)), dma((chunks,)), dma((3,)), dma((3,)), dma((chunks,)), dma((chunks,)), dma, dma]
         + [dma((n_ctx,))] * 2
         + [dma((n_ctx, chunks))] * 2
-        + [dma((n_dp, chunks))] * 2,
+        + [dma((n_dp,))] * 2,
         compiler_params=pltpu.CompilerParams(
             collective_id=0, has_side_effects=True, vmem_limit_bytes=60 * 1024 * 1024),
     )(cotangent.reshape(block), activations.reshape(block), gate_values.reshape(block),

time: 45.8 us -> 44.3 us (0.967)
  Pallas kernels: 41.3 us -> 39.8 us
    pallas_call x1, Pallas kernels: 41.3 us -> 39.8 us  [on_device(): pl.pallas_call(functools.partial(kernel, sizes), out_shape=(jax.ShapeDtyp...]
where the time goes in v2:
time: 44.3 us; the launch traced here: 44 us
  Pallas kernels  39.8 us (90%)
  local copies, waits for them, and re-layouts  3.63 us (8%)
  between operations  0.65 us (1%)
    pallas_call x1, Pallas kernels, on_device(): pl.pallas_call(functools.partial(kernel, sizes), out_shape=(jax.ShapeDtyp...  39.8 us
    unnamed x7, local copies, waits for them, and re-layouts  3.63 us

profile of v2, /device:TPU:0, one launch (start us, length us, event | category | flops | bytes accessed | tf_op | source)
XLA Modules:
  0.0 44.0 jit_solution(4834414798154122242)
XLA Ops:
  0.6 39.8 %shard_map.85 = (bf16[128,4096]{1,0:T(8,128)(2,1)}, f32[1,4096]{1,0:T(1,128)}, f32[1,4096]{1,0:T(1,128)}) custom-call(bf16[128,4096]{1,0:T(8,128)(2,1)} %bitcast.4, bf16[128,4096]{1,0:T(8,128)(2,1)} %bitcast.5, bf16[128,4096]{1,0:T(8,128)(2,1)} %bitcast.6, f32[1,4096]{1,0:T(1,128)} %residue_h.1, f32[1,4096]{1,0:T(1,128)} %skip_h.1, f32[1,4096]{1,0:T(1,128)} %rate_h.1), custom_call_target="tpu_custom_call" | custom-call | tf_op jit(solution)/shard_map/pallas_call | solution.py:338
  40.4 0.0 copy-start.1
  40.4 2.3 %copy.12 = bf16[1,1,128,4096]{3,2,1,0:T(8,128)(2,1)} copy(bf16[1,1,128,4096]{3,2,1,0:T(8,128)(2,1)} %bitcast.7) | data formatting | bytes 2097152
  42.7 0.0 copy-done.1
  42.7 0.0 copy-start
  42.7 0.6 %copy.13 = f32[1,4096]{1,0:T(1,128)} copy(f32[1,4096]{1,0:T(1,128)S(1)} %copy-done.1) | data formatting | bytes 32768
  43.3 0.1 copy-done
  43.4 0.6 %copy.14 = f32[1,4096]{1,0:T(1,128)} copy(f32[1,4096]{1,0:T(1,128)S(1)} %copy-done) | data formatting | bytes 32768
Async XLA Ops:
  40.4 2.3 %copy-start.1 = (f32[1,4096]{1,0:T(1,128)S(1)}, f32[1,4096]{1,0:T(1,128)}, u32[]{:S(2)}) copy-start(f32[1,4096]{1,0:T(1,128)} %get-tuple-element.13) | copy-start | bytes 49156
  42.7 0.7 %copy-start = (f32[1,4096]{1,0:T(1,128)S(1)}, f32[1,4096]{1,0:T(1,128)}, u32[]{:S(2)}) copy-start(f32[1,4096]{1,0:T(1,128)} %get-tuple-element.14) | copy-start | bytes 49156
